TPU v7x, 32 devices: a whole 2x2x4 slice. The times are simulated.
32 devices in a mesh: row: 4 (over y, core), col: 8 (over z, x).
Axes of the slice: x: 2, y: 2, z: 4, core: 2. Of those that a mesh axis runs over, the one named last changes fastest.
Arguments:
- jacobian: bfloat16 [4096, 512], P('row', 'col'), may hold values from -6 to 6
- gram_old: float32 [4096, 4096], P('row', 'col'), may hold values from -1 to 5, as said below
Outputs:
- gram_new: float32 [4096, 4096], P('row', 'col')
- panel_t: float32 [1024, 4096], P('col', 'row')
Inputs may be any that keep to these rules, and one draw needn't show every extreme that they name: `gram_old`: symmetric and positive definite with smallest eigenvalue at least 0.5; diagonal entries between 1 and 5, off-diagonal entries at most 4 / sqrt(4096) in magnitude.
All inputs are finite; a program needn't handle non-finite values.
Results may differ from a plain program's by a relative error of at most 0.0003.
Values may be sent and summed in bfloat16 or wider, within the bound.
A program may use at most 128 MiB of HBM per device.

v0:
```python
import jax
import jax.numpy as jnp
from jax import lax
from jax.sharding import PartitionSpec as P

PARAMS = 512
PANEL = 1024


def broadcast(value, axis, source):
    kept = jnp.where(lax.axis_index(axis) == source, value, 0).astype(value.dtype)
    return lax.psum(kept, axis)


def body(jacobian, gram_old):
    slab_rows = lax.all_gather(jacobian, "col", axis=1, tiled=True)
    tile_rows = gram_old.shape[0]
    tile_cols = gram_old.shape[1]
    row_index = lax.axis_index("row")
    col_index = lax.axis_index("col")
    col_start = col_index * tile_cols
    owner_row = col_start // tile_rows
    offset = col_start % tile_rows
    own_piece = lax.dynamic_slice_in_dim(slab_rows, offset, tile_cols, 0)
    partner = broadcast(own_piece, "row", owner_row)
    row_ids = row_index * tile_rows + jnp.arange(tile_rows, dtype=jnp.int32)
    col_ids = col_start + jnp.arange(tile_cols, dtype=jnp.int32)
    keep_mask = col_ids[None, :] // PANEL <= row_ids[:, None] // PANEL
    active = col_start // PANEL <= ((row_index + 1) * tile_rows - 1) // PANEL

    def tile_product():
        return lax.dot_general(
            slab_rows, partner, (((1,), (1,)), ((), ())), preferred_element_type=jnp.float32
        )

    def tile_zeros():
        return jnp.zeros((tile_rows, tile_cols), jnp.float32)

    product = lax.cond(active, tile_product, tile_zeros)
    gram_new = jnp.where(keep_mask, gram_old + product / PARAMS, gram_old)
    panel_tiles_count = PANEL // tile_cols
    identity = jnp.eye(PANEL, dtype=jnp.float32)
    blocks = []
    for tile_number in range(panel_tiles_count):
        received = broadcast(gram_new, ("row", "col"), tile_number)
        blocks.append(received)
    diagonal = jnp.concatenate(blocks, axis=1)
    factor = jnp.linalg.cholesky(diagonal)
    inverse = jax.scipy.linalg.solve_triangular(factor, identity, lower=True)
    own_count = PANEL // lax.axis_size("col")
    pieces = []
    for tile_number in range(panel_tiles_count):
        pieces.append(broadcast(gram_new, "col", tile_number))
    panel_rows = jnp.concatenate(pieces, axis=1)
    own_inverse = lax.dynamic_slice_in_dim(inverse, col_index * own_count, own_count, 0)
    panel_t = lax.dot_general(
        own_inverse,
        panel_rows,
        (((1,), (1,)), ((), ())),
        precision=lax.Precision.HIGHEST,
        preferred_element_type=jnp.float32,
    )
    return (gram_new, panel_t)


def solution(mesh):
    return jax.shard_map(
        body,
        mesh=mesh,
        in_specs=(P("row", "col"), P("row", "col")),
        out_specs=(P("row", "col"), P("col", "row")),
        check_vma=False,
    )
```

profile of v0, /device:TPU:0, one launch (start us, length us, event | category | flops | bytes accessed | tf_op | source)
XLA Modules:
  0.0 611.8 jit_solution(2063477192917117973)
XLA Ops:
  8.0 45.0 %all-gather.2.cloned.1.call-done = bf16[1024,512]{0,1:T(8,128)(2,1)} async-done(((bf16[1024,64]{0,1:T(8,128)(2,1)}), bf16[1024,512]{0,1:T(8,128)(2,1)}) %all-gather.2.cloned.1.call-update) | async-done | bytes 1048592 | tf_op jit(solution)/shard_map/all_gather | solution.py:16
  53.0 2.0 dynamic-slice_select_fusion
  55.1 2.9 copy.13
  58.0 29.9 %all-reduce.7.cloned.1.call-done = bf16[512,512]{0,1:T(8,128)(2,1)} async-done(((bf16[512,512]{0,1:T(8,128)(2,1)}), bf16[512,512]{0,1:T(8,128)(2,1)}) %all-reduce.7.cloned.1.call-update) | async-done | bytes 524304 | tf_op jit(solution)/shard_map/psum | solution.py:12
  87.9 1.8 conditional.1
  87.9 1.8 fusion.84
  91.1 3.9 broadcast_select_fusion.2
  95.0 2.8 broadcast_select_fusion.3
  98.2 2.4 fusion.25
  100.7 1.8 copy.16
  102.5 136.5 %all-reduce.9.cloned.1.call-done = (f32[1024,512]{0,1:T(8,128)}, f32[1024,512]{0,1:T(8,128)}) async-done(((f32[1024,512]{0,1:T(8,128)}, f32[1024,512]{0,1:T(8,128)}), (f32[1024,512]{0,1:T(8,128)}, f32[1024,512]{0,1:T(8,128)})) %all-reduce.9.cloned.1.call-update) | async-done | bytes 4194320 | tf_op jit(solution)/shard_map/psum | solution.py:12
  239.0 3.3 constant_dynamic-update-slice_fusion.1
  242.3 1.5 constant_dynamic-update-slice_fusion
  243.8 5.6 copy.15
  249.3 4.4 fusion.4
  253.8 2.0 copy-done.1
  255.8 11.7 %cholesky.223 = f32[128,128]{1,0:T(8,128)S(1)} custom-call(f32[128,128]{1,0:T(8,128)S(1)} %cholesky.580), custom_call_target="Cholesky" | custom-call | tf_op jit(solution)/shard_map/jit(cholesky)/cholesky | solution.py:48
  267.5 9.8 %custom-call.63 = f32[1,128,128]{1,2,0:T(8,128)S(1)} custom-call(f32[1,128,128]{2,1,0:T(8,128)S(1)} %get-tuple-element.91), custom_call_target="InvertDiagBlocksLowerTriangular" | custom-call | tf_op jit(solution)/shard_map/jit(cholesky)/cholesky | solution.py:48
  277.3 2.5 cholesky.255
  279.8 2.3 constant_dynamic-update-slice_fusion.33
  282.2 1.5 convolution_subtract_fusion.5
  283.7 11.9 %cholesky.244 = f32[128,128]{1,0:T(8,128)S(1)} custom-call(f32[128,128]{1,0:T(8,128)S(1)} %cholesky.584), custom_call_target="Cholesky" | custom-call | tf_op jit(solution)/shard_map/jit(cholesky)/cholesky | solution.py:48
  296.3 9.8 %custom-call.64 = f32[1,128,128]{1,2,0:T(8,128)S(1)} custom-call(f32[1,128,128]{2,1,0:T(8,128)S(1)} %get-tuple-element.88), custom_call_target="InvertDiagBlocksLowerTriangular" | custom-call | tf_op jit(solution)/shard_map/jit(cholesky)/cholesky | solution.py:48
  307.3 2.1 convolution_subtract_fusion.6
  309.5 11.7 %cholesky.468 = f32[128,128]{1,0:T(8,128)S(1)} custom-call(f32[128,128]{1,0:T(8,128)S(1)} %cholesky.589), custom_call_target="Cholesky" | custom-call | tf_op jit(solution)/shard_map/jit(cholesky)/cholesky | solution.py:48
  322.5 9.8 %custom-call.65 = f32[1,128,128]{1,2,0:T(8,128)S(1)} custom-call(f32[1,128,128]{2,1,0:T(8,128)S(1)} %get-tuple-element.85), custom_call_target="InvertDiagBlocksLowerTriangular" | custom-call | tf_op jit(solution)/shard_map/jit(cholesky)/cholesky | solution.py:48
  333.4 2.3 convolution_subtract_fusion.7
  335.8 12.1 %cholesky.487 = f32[128,128]{1,0:T(8,128)S(1)} custom-call(f32[128,128]{1,0:T(8,128)S(1)} %cholesky.594), custom_call_target="Cholesky" | custom-call | tf_op jit(solution)/shard_map/jit(cholesky)/cholesky | solution.py:48
  349.2 9.8 %custom-call.66 = f32[1,128,128]{1,2,0:T(8,128)S(1)} custom-call(f32[1,128,128]{2,1,0:T(8,128)S(1)} %get-tuple-element.82), custom_call_target="InvertDiagBlocksLowerTriangular" | custom-call | tf_op jit(solution)/shard_map/jit(cholesky)/cholesky | solution.py:48
  360.1 2.4 convolution_subtract_fusion.8
  362.5 11.7 %cholesky.506 = f32[128,128]{1,0:T(8,128)S(1)} custom-call(f32[128,128]{1,0:T(8,128)S(1)} %cholesky.599), custom_call_target="Cholesky" | custom-call | tf_op jit(solution)/shard_map/jit(cholesky)/cholesky | solution.py:48
  375.5 9.9 %custom-call.67 = f32[1,128,128]{1,2,0:T(8,128)S(1)} custom-call(f32[1,128,128]{2,1,0:T(8,128)S(1)} %get-tuple-element.79), custom_call_target="InvertDiagBlocksLowerTriangular" | custom-call | tf_op jit(solution)/shard_map/jit(cholesky)/cholesky | solution.py:48
  386.5 2.3 convolution_subtract_fusion.9
  388.8 11.7 %cholesky.526 = f32[128,128]{1,0:T(8,128)S(1)} custom-call(f32[128,128]{1,0:T(8,128)S(1)} %cholesky.604), custom_call_target="Cholesky" | custom-call | tf_op jit(solution)/shard_map/jit(cholesky)/cholesky | solution.py:48
  401.8 9.8 %custom-call.68 = f32[1,128,128]{1,2,0:T(8,128)S(1)} custom-call(f32[1,128,128]{2,1,0:T(8,128)S(1)} %get-tuple-element.76), custom_call_target="InvertDiagBlocksLowerTriangular" | custom-call | tf_op jit(solution)/shard_map/jit(cholesky)/cholesky | solution.py:48
  412.6 2.0 convolution_subtract_fusion.10
  414.7 11.9 %cholesky.546 = f32[128,128]{1,0:T(8,128)S(1)} custom-call(f32[128,128]{1,0:T(8,128)S(1)} %cholesky.609), custom_call_target="Cholesky" | custom-call | tf_op jit(solution)/shard_map/jit(cholesky)/cholesky | solution.py:48
  427.8 9.8 %custom-call.69 = f32[1,128,128]{1,2,0:T(8,128)S(1)} custom-call(f32[1,128,128]{2,1,0:T(8,128)S(1)} %get-tuple-element.73), custom_call_target="InvertDiagBlocksLowerTriangular" | custom-call | tf_op jit(solution)/shard_map/jit(cholesky)/cholesky | solution.py:48
  438.4 1.8 convolution_subtract_fusion.11
  440.3 11.7 %cholesky.564 = f32[128,128]{1,0:T(8,128)S(1)} custom-call(f32[128,128]{1,0:T(8,128)S(1)} %convolution_subtract_fusion.11), custom_call_target="Cholesky" | custom-call | tf_op jit(solution)/shard_map/jit(cholesky)/cholesky | solution.py:48
  459.0 4.8 select_select_fusion
  463.9 27.4 %while.1 = (s32[]{:T(128)}, f32[1024,1024]{1,0:T(8,128)}, s32[8,2]{0,1:T(2,128)S(1)}, f32[8,128,128]{2,1,0:T(8,128)}, s32[]{:T(128)}) while((s32[]{:T(128)}, f32[1024,1024]{1,0:T(8,128)}, s32[8,2]{0,1:T(2,128)S(1)}, f32[8,128,128]{2,1,0:T(8,128)}, s32[]{:T(128)}) %tuple.79), condition=%wide.while_cond, body=%wide.while_body.sunk | while | flops 2 | bytes 132205 | solution.py:49
  464.5 2.8 bitcast_dynamic-update-slice_fusion.2
  467.9 2.8 bitcast_dynamic-update-slice_fusion.2
  471.3 2.8 bitcast_dynamic-update-slice_fusion.2
  474.7 2.8 bitcast_dynamic-update-slice_fusion.2
  478.2 2.8 bitcast_dynamic-update-slice_fusion.2
  481.6 2.8 bitcast_dynamic-update-slice_fusion.2
  485.0 2.8 bitcast_dynamic-update-slice_fusion.2
  488.5 2.8 bitcast_dynamic-update-slice_fusion.2
  491.2 79.8 %custom-call.70 = f32[8,128,128]{1,2,0:T(8,128)S(1)} custom-call(f32[8,128,128]{2,1,0:T(8,128)} %get-tuple-element.18), custom_call_target="InvertDiagBlocksLowerTriangular" | custom-call | tf_op jit(solution)/shard_map/jit(_solve_triangular)/triangular_solve | solution.py:49
  572.4 1.7 convolution_subtract_fusion.4
  574.1 1.6 constant_dynamic-update-slice_fusion.18
  575.8 1.6 convolution_subtract_fusion
  577.4 1.5 constant_dynamic-update-slice_fusion.17
  578.9 2.0 fusion.19
  581.0 1.5 constant_dynamic-update-slice_fusion.16
  582.5 2.2 fusion.22
  584.7 1.5 constant_dynamic-update-slice_fusion.15
  586.3 2.6 convolution_subtract_fusion.2
  588.9 1.5 constant_dynamic-update-slice_fusion.14
  590.4 2.8 convolution_subtract_fusion.1
  594.7 3.4 convolution_subtract_fusion.3
  599.5 5.6 fusion
  (71 shorter events, 27.2 us)
Async XLA Ops:
  7.2 45.9 %all-gather.2.cloned.1.call-start = ((), (), s32[]{:S(2)}) async-start(), calls=%async_computation | async-start | bytes 1179648 | tf_op jit(solution)/shard_map/all_gather | solution.py:16
  7.9 80.0 %all-reduce.7.cloned.1.call-start = ((), (), s32[]{:S(2)}) async-start(), calls=%async_computation.1 | async-start | bytes 1048576 | tf_op jit(solution)/shard_map/psum | solution.py:12
  53.0 34.9 %copy-start.3 = (bf16[1024,512]{0,1:T(8,128)(2,1)S(1)}, bf16[1024,512]{0,1:T(8,128)(2,1)}, u32[]{:S(2)}) copy-start(bf16[1024,512]{0,1:T(8,128)(2,1)} %all-gather.2.cloned.1.call-done) | copy-start | bytes 3145732
  55.1 183.9 %all-reduce.9.cloned.1.call-start = ((), (), s32[]{:S(2)}) async-start(), calls=%async_computation.2 | async-start | bytes 8388608 | tf_op jit(solution)/shard_map/psum | solution.py:12
  89.7 1.4 copy-start.2
  97.8 501.7 %all-reduce.11.cloned.1.call-start = ((), (), s32[]{:S(2)}) async-start(), calls=%async_computation.3 | async-start | bytes 8388608 | tf_op jit(solution)/shard_map/psum | solution.py:12
  239.0 3.3 copy-start.4
  253.8 2.0 copy-start.1
  571.0 4.7 copy-start
Sparse Core Ops, SparseCore 0:
  10.1 42.8 all-gather.1
  55.9 31.9 all-reduce.6
  98.0 140.9 all-reduce.8
  242.5 156.3 all-reduce.10
where the time goes:
time: 617 us; the launch traced here: 612 us
  other arithmetic  273 us (44%)
  waiting for transfers between devices  212 us (34%)
  matrix products  58.9 us (10%)
  local copies, waits for them, and re-layouts  48.3 us (8%)
  between operations  19.3 us (3%)
    another operation x30, other arithmetic, body(): factor = jnp.linalg.cholesky(diagonal)  172 us
    psum x3, waiting for transfers between devices, broadcast(): return lax.psum(kept, axis)  166 us
    another operation x3, other arithmetic, body(): inverse = jax.scipy.linalg.solve_triangular(factor, identity, lower=True)  84.6 us
    all_gather x1, waiting for transfers between devices, body(): slab_rows = lax.all_gather(jacobian, 'col', axis=1, tiled=True)  45 us
    another operation x15, matrix products, body(): inverse = jax.scipy.linalg.solve_triangular(factor, identity, lower=True)  28.4 us
    another operation x24, local copies, waits for them, and re-layouts  27.4 us
    another operation x14, matrix products, body(): factor = jnp.linalg.cholesky(diagonal)  23.1 us
  transfers between devices with their start and end apart: 4, of which 3 were waited for; matrix products, arithmetic and copies ran while one was open for 59% of the time, Pallas kernels for 0%

commit v1 on v0

--- a/solution.py
+++ b/solution.py
@@ -1,10 +1,113 @@
+import functools
 import jax
 import jax.numpy as jnp
 from jax import lax
+from jax.experimental import pallas as pl
+from jax.experimental.pallas import tpu as pltpu
 from jax.sharding import PartitionSpec as P
 
 PARAMS = 512
 PANEL = 1024
+BLOCK = 128
+
+
+def split3(x):
+    high = x.astype(jnp.bfloat16).astype(jnp.float32)
+    rest = x - high
+    mid = rest.astype(jnp.bfloat16).astype(jnp.float32)
+    return high, mid, rest - mid
+
+
+def left6(x, axis):
+    h, m, l = split3(x)
+    return jnp.concatenate([h, h, m, h, l, m], axis=axis).astype(jnp.bfloat16)
+
+
+def right6(x):
+    h, m, l = split3(x)
+    return jnp.concatenate([h, m, h, l, h, m], axis=0).astype(jnp.bfloat16)
+
+
+def dot_t(a, b):
+    return lax.dot_general(a, b, (((0,), (0,)), ((), ())), preferred_element_type=jnp.float32)
+
+
+def eliminate(work, sub):
+    size = work.shape[0]
+    lanes = lax.broadcasted_iota(jnp.int32, (sub, size), 1)
+    subs = lax.broadcasted_iota(jnp.int32, (sub, size), 0)
+    for start in range(0, size, sub):
+        rows = work[start:start + sub, :]
+        scale = jnp.ones((sub, size), jnp.float32)
+        for i in range(sub):
+            at = start + i
+            column = jnp.broadcast_to(rows[:, at:at + 1], (sub, size))
+            pivot = jnp.broadcast_to(column[i:i + 1, :], (sub, size))
+            pivot_row = jnp.where(lanes == at, 1.0, jnp.broadcast_to(rows[i:i + 1, :], (sub, size)))
+            factor = jnp.where(subs > i, column * (1.0 / pivot), 0.0)
+            kept = jnp.where((lanes == at) & (subs >= i), jnp.where(subs == i, 1.0, 0.0), rows)
+            rows = kept - factor * pivot_row
+            root = lax.rsqrt(pivot)
+            root = root * (1.5 - 0.5 * pivot * root * root)
+            scale = jnp.where(subs == i, root, scale)
+        rows = rows * scale
+        work[start:start + sub, :] = rows
+        low = start + sub
+        if low < size:
+            above = (lanes > subs + start) & (lanes < low)
+            update = dot_t(left6(rows, 0), right6(jnp.where(above, 0.0, rows)))
+            wide = lax.broadcasted_iota(jnp.int32, (size - low, size), 1)
+            inside = (wide >= start) & (wide < low)
+            work[low:, :] = jnp.where(inside, 0.0, work[low:, :]) - update[low:, :]
+
+
+def factor_kernel(sub, a_ref, out_ref, work, left, right):
+    size = a_ref.shape[0]
+    count = size // BLOCK
+    out_ref[...] = a_ref[...]
+
+    def step(k, carry):
+        here = pl.ds(pl.multiple_of(k * BLOCK, BLOCK), BLOCK)
+        work[...] = out_ref[here, here]
+        eliminate(work, sub)
+        r = lax.broadcasted_iota(jnp.int32, (BLOCK, BLOCK), 0)
+        c = lax.broadcasted_iota(jnp.int32, (BLOCK, BLOCK), 1)
+        inverse = jnp.where(c <= r, work[...], 0.0)
+        row = jnp.dot(left6(inverse, 1), right6(out_ref[here, :]), preferred_element_type=jnp.float32)
+        out_ref[here, :] = row
+        out_ref[here, here] = inverse
+        row = out_ref[here, :]
+        left[...] = left6(row, 0)
+        right[...] = right6(row)
+
+        def trail(i, carry):
+            there = pl.ds(pl.multiple_of(i * BLOCK, BLOCK), BLOCK)
+            out_ref[there, here] = jnp.zeros((BLOCK, BLOCK), jnp.float32)
+            out_ref[there, :] = out_ref[there, :] - dot_t(left[:, there], right[...])
+            out_ref[here, there] = jnp.zeros((BLOCK, BLOCK), jnp.float32)
+            return carry
+
+        lax.fori_loop(k + 1, count, trail, 0)
+        return carry
+
+    lax.fori_loop(0, count, step, 0)
+
+
+def inverse_factor(diagonal, sub=16):
+    size = diagonal.shape[0]
+    return pl.pallas_call(
+        functools.partial(factor_kernel, sub),
+        out_shape=jax.ShapeDtypeStruct((size, size), jnp.float32),
+        in_specs=[pl.BlockSpec(memory_space=pltpu.VMEM)],
+        out_specs=pl.BlockSpec(memory_space=pltpu.VMEM),
+        scratch_shapes=[
+            pltpu.VMEM((BLOCK, BLOCK), jnp.float32),
+            pltpu.VMEM((6 * BLOCK, size), jnp.bfloat16),
+            pltpu.VMEM((6 * BLOCK, size), jnp.bfloat16),
+        ],
+        compiler_params=pltpu.CompilerParams(vmem_limit_bytes=40 * 1024 * 1024),
+        cost_estimate=pl.CostEstimate(flops=2 * 10**9, bytes_accessed=2 * 4 * size * size, transcendentals=0),
+    )(diagonal)
 
 
 def broadcast(value, axis, source):
@@ -39,18 +142,17 @@
     product = lax.cond(active, tile_product, tile_zeros)
     gram_new = jnp.where(keep_mask, gram_old + product / PARAMS, gram_old)
     panel_tiles_count = PANEL // tile_cols
-    identity = jnp.eye(PANEL, dtype=jnp.float32)
     blocks = []
     for tile_number in range(panel_tiles_count):
         received = broadcast(gram_new, ("row", "col"), tile_number)
         blocks.append(received)
     diagonal = jnp.concatenate(blocks, axis=1)
-    factor = jnp.linalg.cholesky(diagonal)
-    inverse = jax.scipy.linalg.solve_triangular(factor, identity, lower=True)
+    diagonal, later = lax.optimization_barrier((diagonal, gram_new))
+    inverse = inverse_factor(diagonal)
     own_count = PANEL // lax.axis_size("col")
     pieces = []
     for tile_number in range(panel_tiles_count):
-        pieces.append(broadcast(gram_new, "col", tile_number))
+        pieces.append(broadcast(later, "col", tile_number))
     panel_rows = jnp.concatenate(pieces, axis=1)
     own_inverse = lax.dynamic_slice_in_dim(inverse, col_index * own_count, own_count, 0)
     panel_t = lax.dot_general(

time: 617 us -> 416 us (0.67)
  other arithmetic: 273 us -> 14.9 us
  Pallas kernels: 0 us -> 144 us
  matrix products: 58.9 us -> 9.68 us
  local copies, waits for them, and re-layouts: 48.3 us -> 5.45 us
  waiting for transfers between devices: 212 us -> 228 us
    another operation x33 -> x0, other arithmetic: 257 us -> none  [the longest x30 172 us: body(): factor = jnp.linalg.cholesky(diagonal)]
    pallas_call x0 -> x1, Pallas kernels: none -> 144 us  [inverse_factor(): pl.pallas_call(functools.partial(factor_kernel, sub), out_shape=jax.Shape...]
    another operation x29 -> x0, matrix products: 51.5 us -> none  [the longest x15 28.4 us: body(): inverse = jax.scipy.linalg.solve_triangular(factor, identity, lower=True)]
    another operation x33 -> x0, local copies, waits for them, and re-layouts: 29.9 us -> none
    psum x3, waiting for transfers between devices: 166 us -> 182 us  [broadcast(): return lax.psum(kept, axis)]
    concatenate x2 -> x0, local copies, waits for them, and re-layouts: 7.05 us -> none  [body(): diagonal = jnp.concatenate(blocks, axis=1)]
  transfers between devices with their start and end apart: 4 -> 4, of which waited for: 3 -> 4; matrix products, arithmetic and copies ran while one was open for 59% -> 0% of each run, Pallas kernels for 0% -> 35%
where the time goes in v1:
time: 416 us
  waiting for transfers between devices  228 us (55%)
  Pallas kernels  144 us (35%)
  other arithmetic  14.9 us (4%)
  between operations  13.9 us (3%)
  matrix products  9.68 us (2%)
  local copies, waits for them, and re-layouts  5.45 us (1%)
    psum x3, waiting for transfers between devices, broadcast(): return lax.psum(kept, axis)  182 us
    pallas_call x1, Pallas kernels, inverse_factor(): pl.pallas_call(functools.partial(factor_kernel, sub), out_shape=jax.Shape...  144 us
    all_gather x1, waiting for transfers between devices, body(): slab_rows = lax.all_gather(jacobian, 'col', axis=1, tiled=True)  45 us
    select_n x4, other arithmetic, broadcast(): jnp.where(lax.axis_index(axis) == source, value, 0).astype(value.dtype)  10.2 us
  transfers between devices with their start and end apart: 4, of which 4 were waited for; matrix products, arithmetic and copies ran while one was open for 0% of the time, Pallas kernels for 35%

profile of v1, /device:TPU:0, one launch (start us, length us, event | category | flops | bytes accessed | tf_op | source)
XLA Modules:
  0.0 416.2 jit_solution(13349149063762251332)
XLA Ops:
  7.2 0.0 all-gather.2.cloned.1.call-start
  7.2 0.7 all-gather.2.cloned.1.call-update
  7.9 0.0 all-reduce.6.cloned.1.call-start
  8.0 45.0 %all-gather.2.cloned.1.call-done = bf16[1024,512]{0,1:T(8,128)(2,1)} async-done(((bf16[1024,64]{0,1:T(8,128)(2,1)}), bf16[1024,512]{0,1:T(8,128)(2,1)}) %all-gather.2.cloned.1.call-update) | async-done | bytes 1048592 | tf_op jit(solution)/shard_map/all_gather | solution.py:119
  53.0 1.9 dynamic-slice_select_fusion
  54.9 0.0 all-reduce.6.cloned.1.call-update
  55.0 0.0 all-reduce.8.cloned.1.call-start
  55.1 32.9 %all-reduce.6.cloned.1.call-done = bf16[512,512]{0,1:T(8,128)(2,1)} async-done(((bf16[512,512]{0,1:T(8,128)(2,1)}), bf16[512,512]{0,1:T(8,128)(2,1)}) %all-reduce.6.cloned.1.call-update) | async-done | bytes 524304 | tf_op jit(solution)/shard_map/psum | solution.py:115
  87.9 2.1 conditional.1
  87.9 2.1 fusion.13
  90.0 0.0 copy-start.3
  90.0 1.3 copy-done.3
  91.4 4.0 broadcast_select_fusion.3
  95.3 0.0 copy-start.2
  95.3 1.7 broadcast_select_fusion.2
  97.0 0.0 all-reduce.8.cloned.1.call-update
  97.1 0.0 all-reduce.10.cloned.1.call-start
  97.1 141.1 %all-reduce.8.cloned.1.call-done = (f32[1024,512]{1,0:T(8,128)}, f32[1024,512]{1,0:T(8,128)}) async-done(((f32[1024,512]{1,0:T(8,128)}, f32[1024,512]{1,0:T(8,128)}), (f32[1024,512]{1,0:T(8,128)}, f32[1024,512]{1,0:T(8,128)})) %all-reduce.8.cloned.1.call-update) | async-done | bytes 4194320 | tf_op jit(solution)/shard_map/psum | solution.py:115
  238.2 4.7 %pad_maximum_fusion.a_ref = f32[1024,1024]{1,0:T(8,128)} fusion(f32[1024,512]{1,0:T(8,128)} %get-tuple-element.17, f32[1024,512]{1,0:T(8,128)} %get-tuple-element.18), kind=kLoop, calls=%fused_computation | loop fusion | flops 1048576 | bytes 8388608 | tf_op jit(solution)/shard_map/concatenate | solution.py:149
  242.9 0.0 copy-done.2
  242.9 2.6 broadcast_select_fusion.1
  245.5 0.0 all-reduce.10.cloned.1.call-update
  245.5 0.0 copy-start
  245.5 2.2 copy-done
  247.7 144.2 %shard_map.41 = f32[1024,1024]{1,0:T(8,128)S(1)} custom-call(f32[1024,1024]{1,0:T(8,128)S(1)} %copy-done), custom_call_target="tpu_custom_call" | custom-call | flops 2000000000 | bytes 8388608 | tf_op jit(solution)/shard_map/pallas_call | solution.py:98
  391.9 0.0 copy-start.1
  391.9 1.9 copy-done.1
  393.8 8.2 %all-reduce.10.cloned.1.call-done = (f32[1024,512]{1,0:T(8,128)}, f32[1024,512]{1,0:T(8,128)}) async-done(((f32[1024,512]{1,0:T(8,128)}, f32[1024,512]{1,0:T(8,128)}), (f32[1024,512]{1,0:T(8,128)}, f32[1024,512]{1,0:T(8,128)})) %all-reduce.10.cloned.1.call-update) | async-done | bytes 4194320 | tf_op jit(solution)/shard_map/psum | solution.py:115
  402.0 7.6 %fusion = f32[128,1024]{1,0:T(8,128)} fusion(f32[1024,512]{1,0:T(8,128)} %get-tuple-element.19, f32[1024,512]{1,0:T(8,128)} %get-tuple-element.20, f32[1024,1024]{1,0:T(8,128)} %copy-done.1, s32[]{:T(128)S(6)} %select_n.92), kind=kOutput, calls=%fused_computation.1 | convolution fusion | flops 1611661312 | bytes 5242884 | tf_op jit(solution)/shard_map/dot_general | solution.py:158
  (2 shorter events, 0.0 us)
Async XLA Ops:
  7.2 45.8 %all-gather.2.cloned.1.call-start = ((), (), s32[]{:S(2)}) async-start(), calls=%async_computation | async-start | bytes 1179648 | tf_op jit(solution)/shard_map/all_gather | solution.py:119
  7.9 80.0 %all-reduce.6.cloned.1.call-start = ((), (), s32[]{:S(2)}) async-start(), calls=%async_computation.1 | async-start | bytes 1048576 | tf_op jit(solution)/shard_map/psum | solution.py:115
  55.0 183.2 %all-reduce.8.cloned.1.call-start = ((), (), s32[]{:S(2)}) async-start(), calls=%async_computation.2 | async-start | bytes 8388608 | tf_op jit(solution)/shard_map/psum | solution.py:115
  90.0 1.3 copy-start.3
  95.3 147.6 %copy-start.2 = (f32[1024,512]{1,0:T(8,128)}, f32[1024,512]{1,0:T(8,128)S(1)}, u32[]{:S(2)}) copy-start(f32[1024,512]{1,0:T(8,128)S(1)} %get-tuple-element.14) | copy-start | bytes 6291460
  97.1 305.0 %all-reduce.10.cloned.1.call-start = ((), (), s32[]{:S(2)}) async-start(), calls=%async_computation.3 | async-start | bytes 8388608 | tf_op jit(solution)/shard_map/psum | solution.py:115
  245.5 2.2 copy-start
  391.9 2.0 copy-start.1
Sparse Core Ops, SparseCore 0:
  10.1 42.8 all-gather.1
  55.9 31.9 all-reduce.5
  97.2 140.9 all-reduce.7
  245.7 156.3 all-reduce.9

commit v2 on v1

--- a/solution.py
+++ b/solution.py
@@ -61,10 +61,18 @@
             work[low:, :] = jnp.where(inside, 0.0, work[low:, :]) - update[low:, :]
 
 
-def factor_kernel(sub, a_ref, out_ref, work, left, right):
-    size = a_ref.shape[0]
+def factor_kernel(sub, packed_ref, slab_ref, out_ref, work, left, right):
+    size = out_ref.shape[0]
     count = size // BLOCK
-    out_ref[...] = a_ref[...]
+    begin = 0
+    for j in range(count):
+        high = (j + 1) * BLOCK
+        part = slice(j * BLOCK, high)
+        product = dot_t(slab_ref[:, :high], slab_ref[:, part])
+        out_ref[:high, part] = packed_ref[begin:begin + high, :] + product / PARAMS
+        if high < size:
+            out_ref[high:, part] = jnp.zeros((size - high, BLOCK), jnp.float32)
+        begin += high
 
     def step(k, carry):
         here = pl.ds(pl.multiple_of(k * BLOCK, BLOCK), BLOCK)
@@ -93,12 +101,11 @@
     lax.fori_loop(0, count, step, 0)
 
 
-def inverse_factor(diagonal, sub=16):
-    size = diagonal.shape[0]
+def inverse_factor(packed, slab, size, sub=16):
     return pl.pallas_call(
         functools.partial(factor_kernel, sub),
         out_shape=jax.ShapeDtypeStruct((size, size), jnp.float32),
-        in_specs=[pl.BlockSpec(memory_space=pltpu.VMEM)],
+        in_specs=[pl.BlockSpec(memory_space=pltpu.VMEM)] * 2,
         out_specs=pl.BlockSpec(memory_space=pltpu.VMEM),
         scratch_shapes=[
             pltpu.VMEM((BLOCK, BLOCK), jnp.float32),
@@ -106,8 +113,10 @@
             pltpu.VMEM((6 * BLOCK, size), jnp.bfloat16),
         ],
         compiler_params=pltpu.CompilerParams(vmem_limit_bytes=40 * 1024 * 1024),
-        cost_estimate=pl.CostEstimate(flops=2 * 10**9, bytes_accessed=2 * 4 * size * size, transcendentals=0),
-    )(diagonal)
+        cost_estimate=pl.CostEstimate(
+            flops=100 * 10**9, bytes_accessed=8 * size * size, transcendentals=0
+        ),
+    )(packed, slab)
 
 
 def broadcast(value, axis, source):
@@ -115,45 +124,50 @@
     return lax.psum(kept, axis)
 
 
+def pack_upper(tile, tile_number):
+    tile_cols = tile.shape[1]
+    parts = []
+    for begin in range(0, tile_cols, BLOCK):
+        high = tile_number * tile_cols + begin + BLOCK
+        parts.append(tile[:high, begin:begin + BLOCK])
+    return jnp.concatenate(parts, axis=0)
+
+
 def body(jacobian, gram_old):
-    slab_rows = lax.all_gather(jacobian, "col", axis=1, tiled=True)
-    tile_rows = gram_old.shape[0]
-    tile_cols = gram_old.shape[1]
+    tile_rows, tile_cols = gram_old.shape
     row_index = lax.axis_index("row")
     col_index = lax.axis_index("col")
+    panel_tiles_count = PANEL // tile_cols
+    place = row_index * lax.axis_size("col") + col_index
+
+    packed = []
+    for tile_number in range(panel_tiles_count):
+        part = pack_upper(gram_old, tile_number)
+        packed.append(jnp.where(place == tile_number, part, 0))
+    packed = lax.psum(jnp.concatenate(packed, axis=0), ("row", "col"))
+
+    slabs = lax.all_gather(jacobian.T, ("row", "col"))
+    slabs = slabs.reshape(lax.axis_size("row"), PARAMS, tile_rows)
+    first = slabs[0][:, :PANEL]
+    own = lax.dynamic_index_in_dim(slabs, row_index, 0, keepdims=False)
     col_start = col_index * tile_cols
-    owner_row = col_start // tile_rows
-    offset = col_start % tile_rows
-    own_piece = lax.dynamic_slice_in_dim(slab_rows, offset, tile_cols, 0)
-    partner = broadcast(own_piece, "row", owner_row)
+    partner = lax.dynamic_slice(
+        slabs, (col_start // tile_rows, 0, col_start % tile_rows), (1, PARAMS, tile_cols)
+    )[0]
+
     row_ids = row_index * tile_rows + jnp.arange(tile_rows, dtype=jnp.int32)
     col_ids = col_start + jnp.arange(tile_cols, dtype=jnp.int32)
     keep_mask = col_ids[None, :] // PANEL <= row_ids[:, None] // PANEL
-    active = col_start // PANEL <= ((row_index + 1) * tile_rows - 1) // PANEL
+    gram_new = jnp.where(keep_mask, gram_old + dot_t(own, partner) / PARAMS, gram_old)
 
-    def tile_product():
-        return lax.dot_general(
-            slab_rows, partner, (((1,), (1,)), ((), ())), preferred_element_type=jnp.float32
-        )
+    inverse = inverse_factor(packed, first, PANEL)
 
-    def tile_zeros():
-        return jnp.zeros((tile_rows, tile_cols), jnp.float32)
-
-    product = lax.cond(active, tile_product, tile_zeros)
-    gram_new = jnp.where(keep_mask, gram_old + product / PARAMS, gram_old)
-    panel_tiles_count = PANEL // tile_cols
-    blocks = []
-    for tile_number in range(panel_tiles_count):
-        received = broadcast(gram_new, ("row", "col"), tile_number)
-        blocks.append(received)
-    diagonal = jnp.concatenate(blocks, axis=1)
-    diagonal, later = lax.optimization_barrier((diagonal, gram_new))
-    inverse = inverse_factor(diagonal)
-    own_count = PANEL // lax.axis_size("col")
+    late, own = lax.optimization_barrier((gram_old, own))
     pieces = []
     for tile_number in range(panel_tiles_count):
-        pieces.append(broadcast(later, "col", tile_number))
-    panel_rows = jnp.concatenate(pieces, axis=1)
+        pieces.append(broadcast(late, "col", tile_number))
+    panel_rows = jnp.concatenate(pieces, axis=1) + dot_t(own, first) / PARAMS
+    own_count = PANEL // lax.axis_size("col")
     own_inverse = lax.dynamic_slice_in_dim(inverse, col_index * own_count, own_count, 0)
     panel_t = lax.dot_general(
         own_inverse,

time: 416 us -> 391 us (0.940)
  waiting for transfers between devices: 228 us -> 199 us
  other arithmetic: 14.9 us -> 6.47 us
  matrix products: 9.68 us -> 16.8 us
    psum x3 -> x1, waiting for transfers between devices: 182 us -> 5.27 us  [broadcast(): return lax.psum(kept, axis)]
    psum x0 -> x1, waiting for transfers between devices: none -> 133 us  [body(): packed = lax.psum(jnp.concatenate(packed, axis=0), ('row', 'col'))]
    all_gather x1, waiting for transfers between devices: 45 us -> 59.8 us  [body(): slabs = lax.all_gather(jacobian.T, ('row', 'col'))]
    select_n x4 -> x1, other arithmetic: 10.2 us -> 2.6 us  [broadcast(): jnp.where(lax.axis_index(axis) == source, value, 0).astype(value.dtype)]
    dot_general x1 -> x2, matrix products: 2.1 us -> 8 us  [dot_t(): lax.dot_general(a, b, (((0,), (0,)), ((), ())), preferred_element_type=jn...]
    slice x0 -> x10, local copies, waits for them, and re-layouts: none -> 5.3 us  [the longest x9 4 us: pack_upper(): parts.append(tile[:high, begin:begin + BLOCK])]
  transfers between devices with their start and end apart: 4 -> 3, of which waited for: 4 -> 3; matrix products, arithmetic and copies ran while one was open for 0% -> 6% of each run, Pallas kernels for 35% -> 37%
where the time goes in v2:
time: 391 us
  waiting for transfers between devices  199 us (51%)
  Pallas kernels  146 us (37%)
  matrix products  16.8 us (4%)
  between operations  13.9 us (4%)
  local copies, waits for them, and re-layouts  9.24 us (2%)
  other arithmetic  6.47 us (2%)
    pallas_call x1, Pallas kernels, inverse_factor(): pl.pallas_call(functools.partial(factor_kernel, sub), out_shape=jax.Shape...  146 us
    psum x1, waiting for transfers between devices, body(): packed = lax.psum(jnp.concatenate(packed, axis=0), ('row', 'col'))  133 us
    all_gather x1, waiting for transfers between devices, body(): slabs = lax.all_gather(jacobian.T, ('row', 'col'))  59.8 us
    dot_general x1, matrix products, body(): lax.dot_general(own_inverse, panel_rows, (((1,), (1,)), ((), ())), precis...  8.79 us
    dot_general x2, matrix products, dot_t(): lax.dot_general(a, b, (((0,), (0,)), ((), ())), preferred_element_type=jn...  8 us
  transfers between devices with their start and end apart: 3, of which 3 were waited for; matrix products, arithmetic and copies ran while one was open for 6% of the time, Pallas kernels for 37%

profile of v2, /device:TPU:0, one launch (start us, length us, event | category | flops | bytes accessed | tf_op | source)
XLA Modules:
  0.0 390.9 jit_solution(5810077517798948164)
XLA Ops:
  7.2 0.0 copy-start.2
  7.2 0.0 all-gather.3.cloned.1.call-start
  7.2 0.7 all-gather.3.cloned.1.call-update
  7.9 0.0 all-reduce.4.cloned.1.call-start
  8.0 1.1 slice.34
  9.0 0.0 copy-done.2
  9.0 0.0 slice-start
  9.0 0.1 slice.33
  9.1 0.8 slice.32
  9.9 0.7 slice.31
  10.6 0.7 slice.30
  11.3 0.7 slice.29
  12.0 1.1 maximum_select_fusion.1
  13.1 0.0 slice-done
  13.1 1.1 maximum_select_fusion
  14.2 1.6 pad_maximum_fusion
  15.9 0.0 all-reduce.4.cloned.1.call-update
  15.9 0.0 all-reduce.6.cloned.1.call-start
  16.0 59.8 %all-gather.3.cloned.1.call-done = bf16[2048,1024]{1,0:T(8,128)(2,1)} async-done(((bf16[64,1024]{1,0:T(8,128)(2,1)}), bf16[2048,1024]{1,0:T(8,128)(2,1)}) %all-gather.3.cloned.1.call-update) | async-done | bytes 4194320 | tf_op jit(solution)/shard_map/all_gather | solution.py:149
  75.8 2.3 dynamic-slice_bitcast_fusion
  78.1 2.6 broadcast_select_fusion.1
  80.7 0.0 all-reduce.6.cloned.1.call-update
  80.7 1.3 slice.38.slab_ref
  82.0 133.0 %all-reduce.4.cloned.1.call-done.packed_ref = f32[4608,128]{1,0:T(8,128)} async-done(((f32[4608,128]{1,0:T(8,128)}), f32[4608,128]{1,0:T(8,128)}) %all-reduce.4.cloned.1.call-update) | async-done | bytes 2359312 | tf_op jit(solution)/shard_map/psum | solution.py:147
  215.0 0.0 copy-start.1
  215.0 1.7 copy-done.1
  216.7 0.0 copy-start.3
  216.7 145.6 %shard_map.41 = f32[1024,1024]{1,0:T(8,128)S(1)} custom-call(f32[4608,128]{1,0:T(8,128)S(1)} %copy-done.1, bf16[512,1024]{1,0:T(8,128)(2,1)S(1)} %slice.38.slab_ref), custom_call_target="tpu_custom_call" | custom-call | flops 99999997952 | bytes 8388608 | tf_op jit(solution)/shard_map/pallas_call | solution.py:105
  362.3 0.0 copy-done.3
  362.3 0.0 copy-start
  362.3 3.5 add_select_fusion
  365.8 0.0 copy-done
  365.8 4.5 %fusion.18 = f32[1024,1024]{1,0:T(8,128)} fusion(bf16[512,1024]{1,0:T(8,128)(2,1)S(1)} %copy-done.3, bf16[2048,1024]{1,0:T(8,128)(2,1)} %all-gather.3.cloned.1.call-done), kind=kOutput, calls=%fused_computation.38 | convolution fusion | flops 1073741824 | bytes 6291456 | tf_op jit(solution)/shard_map/dot_general | solution.py:32
  370.3 5.3 %all-reduce.6.cloned.1.call-done = (f32[1024,512]{1,0:T(8,128)}, f32[1024,512]{1,0:T(8,128)}) async-done(((f32[1024,512]{1,0:T(8,128)}, f32[1024,512]{1,0:T(8,128)}), (f32[1024,512]{1,0:T(8,128)}, f32[1024,512]{1,0:T(8,128)})) %all-reduce.6.cloned.1.call-update) | async-done | bytes 4194320 | tf_op jit(solution)/shard_map/psum | solution.py:124
  375.6 8.8 %fusion = f32[128,1024]{1,0:T(8,128)} fusion(f32[1024,512]{1,0:T(8,128)} %get-tuple-element.6, f32[1024,512]{1,0:T(8,128)} %get-tuple-element.7, f32[1024,1024]{1,0:T(8,128)} %fusion.18, f32[1024,1024]{1,0:T(8,128)} %copy-done, s32[]{:T(128)S(6)} %select_n.90), kind=kOutput, calls=%fused_computation.1 | convolution fusion | flops 1613758464 | bytes 9437188 | tf_op jit(solution)/shard_map/dot_general | solution.py:172
  (3 shorter events, 0.0 us)
Async XLA Ops:
  7.2 1.9 copy-start.2
  7.2 68.7 %all-gather.3.cloned.1.call-start = ((), (), s32[]{:S(2)}) async-start(), calls=%async_computation.1 | async-start | bytes 4325376 | tf_op jit(solution)/shard_map/all_gather | solution.py:149
  7.9 207.1 %all-reduce.4.cloned.1.call-start = ((), (), s32[]{:S(2)}) async-start(), calls=%async_computation | async-start | bytes 4718592 | tf_op jit(solution)/shard_map/psum | solution.py:147
  9.0 4.1 %slice-start = ((f32[1024,512]{1,0:T(8,128)}), f32[1024,128]{1,0:T(8,128)S(1)}, s32[]{:S(2)}) async-start(f32[1024,512]{1,0:T(8,128)} %param.3), calls=%async_computation.3 | async-start | bytes 1048576 | tf_op jit(solution)/shard_map/slice | solution.py:132
  15.9 359.7 %all-reduce.6.cloned.1.call-start = ((), (), s32[]{:S(2)}) async-start(), calls=%async_computation.2 | async-start | bytes 8388608 | tf_op jit(solution)/shard_map/psum | solution.py:124
  215.0 1.7 copy-start.1
  216.7 145.6 %copy-start.3 = (bf16[512,1024]{1,0:T(8,128)(2,1)S(1)}, bf16[512,1024]{1,0:T(8,128)(2,1)}, u32[]{:S(2)}) copy-start(bf16[512,1024]{1,0:T(8,128)(2,1)} %dynamic-slice_bitcast_fusion) | copy-start | bytes 3145732
  362.3 3.5 copy-start
Sparse Core Ops, SparseCore 0:
  11.0 64.7 all-gather.2
  81.4 133.5 all-reduce.3
  219.2 156.3 all-reduce.5

commit v3 on v2

--- a/solution.py
+++ b/solution.py
@@ -138,13 +138,17 @@
     row_index = lax.axis_index("row")
     col_index = lax.axis_index("col")
     panel_tiles_count = PANEL // tile_cols
-    place = row_index * lax.axis_size("col") + col_index
 
     packed = []
     for tile_number in range(panel_tiles_count):
         part = pack_upper(gram_old, tile_number)
-        packed.append(jnp.where(place == tile_number, part, 0))
-    packed = lax.psum(jnp.concatenate(packed, axis=0), ("row", "col"))
+        packed.append(jnp.where(col_index == tile_number, part, 0))
+    packed = jnp.concatenate(packed, axis=0)
+    packed = packed.reshape(lax.axis_size("col"), -1, BLOCK)
+    share = lax.all_to_all(packed, "col", 0, 0)
+    share = jnp.sum(share[:panel_tiles_count], axis=0)
+    share = broadcast(share, "row", 0)
+    packed = lax.all_gather(share, "col", axis=0, tiled=True)
 
     slabs = lax.all_gather(jacobian.T, ("row", "col"))
     slabs = slabs.reshape(lax.axis_size("row"), PARAMS, tile_rows)

time: 391 us -> 373 us (0.954)
  waiting for transfers between devices: 199 us -> 171 us
  starting transfers between devices: 0.12 us -> 7.41 us
    psum x1 -> x0, waiting for transfers between devices: 133 us -> none  [body(): packed = lax.psum(jnp.concatenate(packed, axis=0), ('row', 'col'))]
    all_to_all x0 -> x1, waiting for transfers between devices: none -> 53.9 us  [body(): share = lax.all_to_all(packed, 'col', 0, 0)]
    all_gather x0 -> x1, waiting for transfers between devices: none -> 42.1 us  [body(): packed = lax.all_gather(share, 'col', axis=0, tiled=True)]
    psum x1 -> x2, waiting for transfers between devices: 5.27 us -> 42.2 us  [broadcast(): return lax.psum(kept, axis)]
    all_gather x1, waiting for transfers between devices: 59.8 us -> 32 us  [body(): slabs = lax.all_gather(jacobian.T, ('row', 'col'))]
    all_to_all x0 -> x1, starting transfers between devices: none -> 7.25 us  [body(): share = lax.all_to_all(packed, 'col', 0, 0)]
  transfers between devices with their start and end apart: 3 -> 5, of which waited for: 3 -> 5; matrix products, arithmetic and copies ran while one was open for 6% -> 3% of each run, Pallas kernels for 37% -> 39%
where the time goes in v3:
time: 373 us; the launch traced here: 372 us
  waiting for transfers between devices  171 us (46%)
  Pallas kernels  146 us (39%)
  between operations  15.9 us (4%)
  matrix products  15.3 us (4%)
  local copies, waits for them, and re-layouts  10.1 us (3%)
  starting transfers between devices  7.41 us (2%)
  other arithmetic  7.24 us (2%)
    pallas_call x1, Pallas kernels, inverse_factor(): pl.pallas_call(functools.partial(factor_kernel, sub), out_shape=jax.Shape...  146 us
    all_to_all x1, waiting for transfers between devices, body(): share = lax.all_to_all(packed, 'col', 0, 0)  53.9 us
    psum x2, waiting for transfers between devices, broadcast(): return lax.psum(kept, axis)  42.2 us
    all_gather x1, waiting for transfers between devices, body(): packed = lax.all_gather(share, 'col', axis=0, tiled=True)  42.1 us
    all_gather x1, waiting for transfers between devices, body(): slabs = lax.all_gather(jacobian.T, ('row', 'col'))  32 us
    dot_general x1, matrix products, body(): lax.dot_general(own_inverse, panel_rows, (((1,), (1,)), ((), ())), precis...  8.79 us
  transfers between devices with their start and end apart: 5, of which 5 were waited for; matrix products, arithmetic and copies ran while one was open for 3% of the time, Pallas kernels for 39%

profile of v3, /device:TPU:0, one launch (start us, length us, event | category | flops | bytes accessed | tf_op | source)
XLA Modules:
  0.0 372.4 jit_solution(10058044042638704085)
XLA Ops:
  8.0 0.0 copy-start.2
  8.0 0.0 slice-start
  8.0 1.2 slice.37
  9.2 1.0 slice.36
  10.3 0.0 copy-done.2
  10.3 0.8 slice.35
  11.0 0.7 slice.34
  11.8 0.7 slice.33
  12.5 0.7 slice.32
  13.2 0.0 slice-done
  13.2 0.0 copy-start.4
  13.2 0.0 copy-start.5
  13.2 0.0 copy-start.6
  13.2 1.1 maximum_select_fusion
  14.3 0.0 copy-done.4
  14.4 0.0 copy-done.5
  14.4 0.0 copy-done.6
  14.4 1.6 pad_maximum_fusion
  16.0 7.3 %all-to-all-start = ((f32[8,576,128]{2,1,0:T(8,128)}), f32[8,576,128]{2,1,0:T(8,128)}, u32[]{:S(2)}, u32[]{:S(2)}) async-start(f32[8,576,128]{2,1,0:T(8,128)} %bitcast.10), calls=%async_computation | async-start | bytes 4718592 | tf_op jit(solution)/shard_map/all_to_all | solution.py:148
  23.2 0.0 all-reduce.4.cloned.1.call-start
  23.3 53.9 %all-to-all-done = f32[8,576,128]{2,1,0:T(8,128)} async-done(((f32[8,576,128]{2,1,0:T(8,128)}), f32[8,576,128]{2,1,0:T(8,128)}, u32[]{:S(2)}, u32[]{:S(2)}) %all-to-all-start) | async-done | bytes 2359328 | tf_op jit(solution)/shard_map/all_to_all | solution.py:148
  77.2 1.1 slice_reduce_fusion
  78.4 0.7 broadcast_select_fusion.2
  79.1 0.0 all-reduce.4.cloned.1.call-update
  79.1 0.0 all-gather.6.cloned.1.call-start
  79.2 0.5 all-gather.6.cloned.1.call-update
  79.7 0.0 all-gather.4.cloned.1.call-start
  79.7 31.8 %all-reduce.4.cloned.1.call-done = f32[576,128]{1,0:T(8,128)} async-done(((f32[576,128]{1,0:T(8,128)}), f32[576,128]{1,0:T(8,128)}) %all-reduce.4.cloned.1.call-update) | async-done | bytes 294928 | tf_op jit(solution)/shard_map/psum | solution.py:124
  111.6 0.0 all-gather.4.cloned.1.call-update
  111.6 0.0 all-reduce.6.cloned.1.call-start
  111.7 32.0 %all-gather.6.cloned.1.call-done = bf16[2048,1024]{1,0:T(8,128)(2,1)} async-done(((bf16[64,1024]{1,0:T(8,128)(2,1)}), bf16[2048,1024]{1,0:T(8,128)(2,1)}) %all-gather.6.cloned.1.call-update) | async-done | bytes 4194320 | tf_op jit(solution)/shard_map/all_gather | solution.py:153
  143.8 1.3 dynamic-slice_bitcast_fusion
  145.1 2.6 broadcast_select_fusion.1
  147.6 0.0 all-reduce.6.cloned.1.call-update
  147.7 0.0 copy-start.3
  147.7 3.3 add_select_fusion
  151.0 0.0 copy-done.3
  151.0 0.1 slice.43.slab_ref
  151.0 3.3 fusion.18
  154.3 42.1 %all-gather.4.cloned.1.call-done.packed_ref = f32[4608,128]{1,0:T(8,128)} async-done(((f32[576,128]{1,0:T(8,128)}), f32[4608,128]{1,0:T(8,128)}) %all-gather.4.cloned.1.call-update) | async-done | bytes 2359312 | tf_op jit(solution)/shard_map/all_gather | solution.py:151
  196.4 0.0 copy-start.1
  196.4 1.7 copy-done.1
  198.0 145.6 %shard_map.41 = f32[1024,1024]{1,0:T(8,128)S(1)} custom-call(f32[4608,128]{1,0:T(8,128)S(1)} %copy-done.1, bf16[512,1024]{1,0:T(8,128)(2,1)S(1)} %slice.43.slab_ref), custom_call_target="tpu_custom_call" | custom-call | flops 99999997952 | bytes 8388608 | tf_op jit(solution)/shard_map/pallas_call | solution.py:105
  343.6 0.0 copy-start
  343.6 2.0 copy-done
  345.6 10.4 %all-reduce.6.cloned.1.call-done = (f32[1024,512]{1,0:T(8,128)}, f32[1024,512]{1,0:T(8,128)}) async-done(((f32[1024,512]{1,0:T(8,128)}, f32[1024,512]{1,0:T(8,128)}), (f32[1024,512]{1,0:T(8,128)}, f32[1024,512]{1,0:T(8,128)})) %all-reduce.6.cloned.1.call-update) | async-done | bytes 4194320 | tf_op jit(solution)/shard_map/psum | solution.py:124
  356.0 8.8 %fusion = f32[128,1024]{1,0:T(8,128)} fusion(f32[1024,512]{1,0:T(8,128)} %get-tuple-element.6, f32[1024,512]{1,0:T(8,128)} %get-tuple-element.7, f32[1024,1024]{1,0:T(8,128)} %fusion.18, f32[1024,1024]{1,0:T(8,128)} %copy-done, s32[]{:T(128)S(6)} %select_n.100), kind=kOutput, calls=%fused_computation.1 | convolution fusion | flops 1613758464 | bytes 9437188 | tf_op jit(solution)/shard_map/dot_general | solution.py:176
  (4 shorter events, 0.1 us)
Async XLA Ops:
  8.0 2.3 copy-start.2
  8.0 5.1 %slice-start = ((f32[1024,512]{1,0:T(8,128)}), f32[1024,128]{1,0:T(8,128)S(1)}, s32[]{:S(2)}) async-start(f32[1024,512]{1,0:T(8,128)} %param.3), calls=%async_computation.5 | async-start | bytes 1048576 | tf_op jit(solution)/shard_map/slice | solution.py:132
  13.2 1.2 copy-start.4
  13.2 1.2 copy-start.5
  13.2 1.2 copy-start.6
  16.0 61.2 %all-to-all-start = ((f32[8,576,128]{2,1,0:T(8,128)}), f32[8,576,128]{2,1,0:T(8,128)}, u32[]{:S(2)}, u32[]{:S(2)}) async-start(f32[8,576,128]{2,1,0:T(8,128)} %bitcast.10), calls=%async_computation | async-start | bytes 4718592 | tf_op jit(solution)/shard_map/all_to_all | solution.py:148
  23.2 88.3 %all-reduce.4.cloned.1.call-start = ((), (), s32[]{:S(2)}) async-start(), calls=%async_computation.1 | async-start | bytes 589824 | tf_op jit(solution)/shard_map/psum | solution.py:124
  79.1 64.6 %all-gather.6.cloned.1.call-start = ((), (), s32[]{:S(2)}) async-start(), calls=%async_computation.3 | async-start | bytes 4325376 | tf_op jit(solution)/shard_map/all_gather | solution.py:153
  79.7 116.7 %all-gather.4.cloned.1.call-start = ((), (), s32[]{:S(2)}) async-start(), calls=%async_computation.2 | async-start | bytes 2654208 | tf_op jit(solution)/shard_map/all_gather | solution.py:151
  111.6 244.4 %all-reduce.6.cloned.1.call-start = ((), (), s32[]{:S(2)}) async-start(), calls=%async_computation.4 | async-start | bytes 8388608 | tf_op jit(solution)/shard_map/psum | solution.py:124
  147.7 3.3 copy-start.3
  196.4 1.7 copy-start.1
  343.6 2.0 copy-start
Sparse Core Ops, SparseCore 0:
  79.2 32.2 all-reduce.3
Sparse Core Ops, SparseCore 1:
  82.6 61.1 all-gather.5
  145.8 50.5 all-gather.3
  200.0 155.9 all-reduce.5
